TPU v7x, 32 devices: a whole 2x2x4 slice. The times are simulated.
32 devices in a mesh: aux: 8 (over y, x, core), sec: 4 (over z).
Axes of the slice: x: 2, y: 2, z: 4, core: 2. Of those that a mesh axis runs over, the one named last changes fastest.
Arguments:
- wavefunction: bfloat16 [4096, 2048], P('sec'), may hold values from -6 to 6
- dressed_ops: bfloat16 [4096, 5120], P('sec', 'aux'), may hold values from -0.09375 to 0.09375
- site_tensor: bfloat16 [4096, 4096], P('sec'), may hold values from -6 to 6
- old_sector: int32 [4096], P('sec'), may hold values from 0 to 15, never falling along the last dimension, each value on 1 to 1024 neighbouring positions
- new_sector: int32 [4096], replicated, may hold values from 0 to 15, never falling along the last dimension, each value on 1 to 1024 neighbouring positions
Outputs:
- sigma: bfloat16 [4096, 2048], P(('sec', 'aux'))
- rotated_ops: bfloat16 [4096, 5120], P('sec', 'aux')
All inputs are finite; a program needn't handle non-finite values.
Results may differ from a plain program's by a relative error of at most 0.0034.
Values may be sent and summed in bfloat16 or wider, within the bound.
A program may use at most 128 MiB of HBM per device.

v0:
```python
import jax
import jax.numpy as jnp
from jax import lax
from jax.sharding import PartitionSpec as P


def body(wavefunction, dressed_ops, site_tensor, old_sector, new_sector):
    local_rows = dressed_ops.shape[0]
    partial_images = lax.dot_general(
        dressed_ops, wavefunction, (((0,), (0,)), ((), ())), preferred_element_type=jnp.float32
    )
    images = lax.psum(partial_images, "sec")
    images = images.astype(jnp.bfloat16)
    owned = local_rows // lax.axis_size("aux")
    terms = jnp.dot(dressed_ops, images, preferred_element_type=jnp.float32)
    totals = lax.psum(terms, "aux")
    sigma = lax.dynamic_slice_in_dim(totals, lax.axis_index("aux") * owned, owned, 0).astype(
        jnp.bfloat16
    )
    offset = new_sector[None, :] - old_sector[:, None]
    allowed = (offset >= 0) & (offset <= 2)
    site_blocks = jnp.where(allowed, site_tensor, jnp.zeros_like(site_tensor))
    rotated = lax.psum_scatter(
        lax.dot_general(
            site_blocks, dressed_ops, (((0,), (0,)), ((), ())), preferred_element_type=jnp.float32
        ),
        "sec",
        scatter_dimension=0,
        tiled=True,
    ).astype(jnp.bfloat16)
    return (sigma, rotated)


def solution(mesh):
    placed = (P("sec", None), P("sec", "aux"), P("sec", None), P("sec"), P())
    return jax.shard_map(
        body,
        mesh=mesh,
        in_specs=placed,
        out_specs=(P(("sec", "aux"), None), P("sec", "aux")),
        check_vma=False,
    )
```

profile of v0, /device:TPU:0, one launch (start us, length us, event | category | flops | bytes accessed | tf_op | source)
XLA Modules:
  0.0 561.1 jit_solution(5693226858930224195)
XLA Ops:
  7.2 0.0 copy-start
  7.2 0.0 reduce-scatter.2.cloned.1.call-start
  7.2 1.3 copy-done
  8.5 12.7 %fusion.2 = f32[4096,640]{1,0:T(8,128)} fusion(bf16[1024,640]{1,0:T(8,128)(2,1)S(1)} %copy-done, bf16[1024,4096]{1,0:T(8,128)(2,1)} %param.7, s32[1024]{0:T(1024)} %param.8, s32[4096]{0:T(1024)} %param.9), kind=kOutput, calls=%fused_computation.4 | convolution fusion | flops 5389680640 | bytes 20205568 | tf_op jit(solution)/shard_map/dot_general | solution.py:24
  21.1 0.0 reduce-scatter.2.cloned.1.call-update
  21.2 7.5 %fusion.13 = f32[640,2048]{1,0:T(8,128)} fusion(bf16[1024,640]{1,0:T(8,128)(2,1)S(1)} %copy-done, bf16[1024,2048]{1,0:T(8,128)(2,1)} %param.5), kind=kOutput, calls=%fused_computation.16 | convolution fusion | flops 2684354560 | bytes 10747904 | tf_op jit(solution)/shard_map/dot_general | solution.py:9
  28.7 343.9 %all-reduce.2 = bf16[640,2048]{1,0:T(8,128)(2,1)} all-reduce(f32[640,2048]{1,0:T(8,128)} %fusion.13), channel_id=1, replica_groups=mesh['aux'=8,'sec'=4] {'sec'}, use_global_device_ids=true, to_apply=%region_0.0 | all-reduce | flops 1310720 | bytes 7864320 | tf_op jit(solution)/shard_map/psum | solution.py:12
  372.6 7.5 %convolution_bitcast_fusion = f32[1024,2048]{0,1:T(8,128)} fusion(bf16[1024,640]{1,0:T(8,128)(2,1)S(1)} %copy-done, bf16[640,2048]{1,0:T(8,128)(2,1)} %all-reduce.2), kind=kOutput, calls=%fused_computation.9 | convolution fusion | flops 2684354560 | bytes 12320768 | tf_op jit(solution)/shard_map/dot_general | solution.py:15
  380.0 169.2 %all-reduce.3 = bf16[1024,2048]{0,1:T(8,128)(2,1)} all-reduce(f32[1024,2048]{0,1:T(8,128)} %convolution_bitcast_fusion), channel_id=1, replica_groups=mesh['aux'=8,'sec'=4] {'aux'}, use_global_device_ids=true, to_apply=%region_1.0 | all-reduce | flops 2097152 | bytes 12582912 | tf_op jit(solution)/shard_map/psum | solution.py:16
  549.3 1.1 dynamic-slice_convert_fusion
  550.4 1.0 copy.7
  551.4 0.0 reduce-scatter.2.cloned.1.call-done
  551.4 2.9 convert_element_type.11
Async XLA Ops:
  7.2 1.3 copy-start
  7.2 544.2 %reduce-scatter.2.cloned.1.call-start = ((), (), s32[]{:S(2)}) async-start(), calls=%async_computation.1 | async-start | bytes 13107200 | tf_op jit(solution)/shard_map/reduce_scatter | solution.py:23
Sparse Core Ops, SparseCore 0:
  21.3 340.7 reduce-scatter.1
where the time goes:
time: 562 us; the launch traced here: 561 us
  blocking collectives  513 us (91%)
  matrix products  27.6 us (5%)
  between operations  14 us (2%)
    psum x1, blocking collectives, body(): images = lax.psum(partial_images, 'sec')  344 us
    psum x1, blocking collectives, body(): totals = lax.psum(terms, 'aux')  169 us
    dot_general x1, matrix products, body(): lax.dot_general(site_blocks, dressed_ops, (((0,), (0,)), ((), ())), prefe...  12.7 us
  transfers between devices with their start and end apart: 1, of which 0 were waited for; matrix products, arithmetic and copies ran while one was open for 3% of the time, Pallas kernels for 0%

commit v1 on v0

v1 whole, which is shorter than its diff:
```python
import functools

import jax
import jax.numpy as jnp
from jax import lax
from jax.experimental import pallas as pl
from jax.experimental.pallas import tpu as pltpu
from jax.sharding import PartitionSpec as P

MESH = pl.DeviceIdType.MESH
CHUNKS = 4


def tdot(a, b):
    return lax.dot_general(a, b, (((0,), (0,)), ((), ())), preferred_element_type=jnp.float32)


def kernel(
    nz, na, w_ref, d_ref, s_ref, old_ref, new_ref, sig_ref, rot_ref,
    wf, sf, df, sm, acc, img, rotacc, keep, msend, mrecv, ssend, srecv, tmp,
    loc, z_s, z_r, dr_s, dl_s, d_r, p_s, p_r, m_s, m_r, x_s, x_r, y_s, y_r,
):
    nc = na // 2
    z = lax.axis_index("sec")
    a = lax.axis_index("aux")
    c = lax.rem(a, 2)
    q = a // 2
    mate = a + 1 - 2 * c
    local = d_ref.shape[0]
    rows = local // na
    width = sf.shape[2]
    cols = w_ref.shape[1]
    step = cols // CHUNKS

    def peer(k):
        return lax.rem(a + 2 * k, na)

    def back(k):
        return lax.rem(a + na - 2 * k, na)

    def part(b):
        return pl.ds(pl.multiple_of(b * rows, rows), rows)

    def block(t):
        return pl.ds(pl.multiple_of(t * width, width), width)

    mine = part(a)

    loads = [
        pltpu.make_async_copy(s_ref.at[mine], sm, loc.at[0]),
        pltpu.make_async_copy(d_ref, df.at[z], loc.at[1]),
        pltpu.make_async_copy(w_ref, wf.at[z], loc.at[2]),
        pltpu.make_async_copy(s_ref.at[:, block(z)], sf.at[z], loc.at[3]),
    ]
    for load in loads:
        load.start()

    barrier = pltpu.get_barrier_semaphore()
    for k in range(1, nz):
        pl.semaphore_signal(barrier, inc=1, device_id={"sec": lax.rem(z + k, nz)}, device_id_type=MESH)
    for k in range(1, nc):
        pl.semaphore_signal(barrier, inc=1, device_id={"aux": peer(k)}, device_id_type=MESH)
    pl.semaphore_signal(barrier, inc=1, device_id={"aux": mate}, device_id_type=MESH)
    pl.semaphore_wait(barrier, nz - 1 + nc - 1 + 1)

    def remote(src, dst, send, recv, where):
        return pltpu.make_async_remote_copy(
            src_ref=src, dst_ref=dst, send_sem=send, recv_sem=recv, device_id=where, device_id_type=MESH
        )

    def z_copy(kind, k):
        t = lax.rem(z + k, nz)
        if kind == 0:
            src, dst = w_ref.at[mine], wf.at[z, mine]
        else:
            src, dst = sm.at[:, block(t)], sf.at[z, mine]
        return remote(src, dst, z_s.at[kind, k], z_r.at[kind, k], {"sec": t})

    full = (wf, sf)

    def z_arrived(kind, k):
        p = lax.rem(z + nz - k, nz)
        ref = full[kind].at[p, mine]
        remote(ref, ref, z_s.at[kind, k], z_r.at[kind, k], {"sec": p}).wait_recv()

    def p_copy(kind, j, k):
        ref = full[kind].at[lax.rem(z + nz - j, nz), mine]
        return remote(ref, ref, p_s.at[kind, j, k], p_r.at[kind, j, k], {"aux": peer(k)})

    def p_arrived(kind, j, k):
        ref = full[kind].at[lax.rem(z + nz - j, nz), part(back(k))]
        remote(ref, ref, p_s.at[kind, j, k], p_r.at[kind, j, k], {"aux": back(k)}).wait_recv()

    def m_copy(kind, j, k):
        ref = full[kind].at[lax.rem(z + nz - j, nz), part(back(k))]
        return remote(ref, ref, m_s.at[kind, j, k], m_r.at[kind, j, k], {"aux": mate})

    def m_arrived(kind, j, k):
        theirs = lax.rem(mate + na - 2 * k, na)
        ref = full[kind].at[lax.rem(z + nz - j, nz), part(theirs)]
        remote(ref, ref, m_s.at[kind, j, k], m_r.at[kind, j, k], {"aux": mate}).wait_recv()

    def spread(kind, j):
        z_arrived(kind, j)
        for k in range(1, nc):
            p_copy(kind, j, k).start()
        m_copy(kind, j, 0).start()

    def relay(kind, j):
        for k in range(1, nc):
            p_arrived(kind, j, k)
            m_copy(kind, j, k).start()

    def landed(kind, j):
        for k in range(nc):
            m_arrived(kind, j, k)

    def d_right(p):
        return remote(df.at[p], df.at[p], dr_s.at[p], d_r.at[p], {"sec": z + 1})

    def d_left(p):
        return remote(df.at[p], df.at[p], dl_s.at[p], d_r.at[p], {"sec": z - 1})

    def d_step(distance):
        @pl.when(z - distance >= 0)
        def _():
            p = z - distance
            remote(df.at[p], df.at[p], dr_s.at[p], d_r.at[p], {"sec": z - 1}).wait_recv()

            @pl.when(z < nz - 1)
            def _():
                d_right(p).start()

        @pl.when(z + distance < nz)
        def _():
            p = z + distance
            remote(df.at[p], df.at[p], dl_s.at[p], d_r.at[p], {"sec": z + 1}).wait_recv()

            @pl.when(z > 0)
            def _():
                d_left(p).start()

    for k in range(1, nz):
        z_copy(0, k).start()
    loads[1].wait()

    @pl.when(z < nz - 1)
    def _():
        d_right(z).start()

    @pl.when(z > 0)
    def _():
        d_left(z).start()

    loads[0].wait()
    for t in range(nz):
        band = pl.ds(t * width, width)
        offset = new_ref[:, band] - old_ref[mine, :]
        allowed = (offset >= 0) & (offset <= 2)
        sm[:, band] = jnp.where(allowed, sm[:, band].astype(jnp.float32), 0.0).astype(jnp.bfloat16)
    for k in range(1, nz):
        z_copy(1, k).start()

    loads[3].wait()

    @pl.loop(0, local // 128)
    def _(i):
        r = pl.ds(pl.multiple_of(i * 128, 128), 128)
        offset = new_ref[:, block(z)] - old_ref[r, :]
        allowed = (offset >= 0) & (offset <= 2)
        sf[z, r, :] = jnp.where(allowed, sf[z, r, :].astype(jnp.float32), 0.0).astype(jnp.bfloat16)

    loads[2].wait()

    def add_images(p, first):
        @pl.loop(0, cols // 512)
        def _(i):
            r = pl.ds(pl.multiple_of(i * 512, 512), 512)
            term = tdot(df[p], wf[p, :, r])
            acc[:, r] = term if first else acc[:, r] + term

    def add_rotated(p, first):
        @pl.loop(0, width // 256)
        def _(i):
            r = pl.ds(pl.multiple_of(i * 256, 256), 256)
            term = tdot(sf[p, :, r], df[p])
            rotacc[r, :] = term if first else rotacc[r, :] + term

    add_images(z, True)
    add_rotated(z, True)

    near = [1, nz - 1] + list(range(2, nz - 1))
    for j in near:
        spread(0, j)
    d_step(1)
    for j in near:
        spread(1, j)
    for j in near:
        relay(0, j)
    for d in range(2, nz):
        d_step(d)
        if d == 2:
            for j in near:
                relay(1, j)
            for j in near:
                landed(0, j)

    for j in range(1, nz):
        add_images(lax.rem(z + nz - j, nz), False)

    @pl.loop(0, CHUNKS)
    def _(i):
        r = pl.ds(pl.multiple_of(i * step, step), step)
        img[:, r] = acc[:, r].astype(jnp.bfloat16)

    def x_copy(i):
        r = pl.ds(i * step, step)
        return remote(msend.at[:, :, r], mrecv.at[:, :, r], x_s.at[i], x_r.at[i], {"aux": mate})

    def y_copy(i, k):
        r = pl.ds(i * step, step)
        return remote(ssend.at[k, :, r], srecv.at[k, :, r], y_s.at[i, k], y_r.at[i, k], {"aux": peer(k)})

    def terms(i):
        r = pl.ds(i * step, step)

        @pl.loop(0, nc)
        def _(b):
            pair = pl.ds(pl.multiple_of(b * 2 * rows, 2 * rows), 2 * rows)
            tmp[...] = jnp.dot(df[z, pair, :], img[:, r], preferred_element_type=jnp.float32)
            keep[b, :, r] = tmp[part(c), :]
            msend[b, :, r] = tmp[part(1 - c), :].astype(jnp.bfloat16)

        x_copy(i).start()

    def combine(i):
        r = pl.ds(i * step, step)
        x_copy(i).wait_recv()
        for k in range(1, nc):
            b = lax.rem(q + k, nc)
            ssend[k, :, r] = (keep[b, :, r] + mrecv[b, :, r].astype(jnp.float32)).astype(jnp.bfloat16)
            y_copy(i, k).start()

    for i in range(CHUNKS):
        terms(i)
        if i > 0:
            combine(i - 1)
    combine(CHUNKS - 1)

    for j in near:
        landed(1, j)
    for j in range(1, nz):
        add_rotated(lax.rem(z + nz - j, nz), False)
    rot_ref[...] = rotacc[...].astype(jnp.bfloat16)

    for i in range(CHUNKS):
        r = pl.ds(i * step, step)
        total = keep[q, :, r] + mrecv[q, :, r].astype(jnp.float32)
        for k in range(1, nc):
            y_copy(i, k).wait_recv()
            total = total + srecv[k, :, r].astype(jnp.float32)
        sig_ref[:, r] = total.astype(jnp.bfloat16)

    for kind in range(2):
        for j in range(1, nz):
            z_copy(kind, j).wait_send()
            for k in range(1, nc):
                p_copy(kind, j, k).wait_send()
            for k in range(nc):
                m_copy(kind, j, k).wait_send()
    for p in range(nz):
        @pl.when((p <= z) & (z < nz - 1))
        def _():
            d_right(p).wait_send()

        @pl.when((p >= z) & (z > 0))
        def _():
            d_left(p).wait_send()
    for i in range(CHUNKS):
        x_copy(i).wait_send()
        for k in range(1, nc):
            y_copy(i, k).wait_send()


def body(nz, na, wavefunction, dressed_ops, site_tensor, old_sector, new_sector):
    local, depth = dressed_ops.shape
    cols = wavefunction.shape[1]
    width = site_tensor.shape[1] // nz
    nc, rows = na // 2, local // na
    bf, f4 = jnp.bfloat16, jnp.float32
    dma = pltpu.SemaphoreType.DMA
    vmem = pl.BlockSpec(memory_space=pltpu.VMEM)
    hbm = pl.BlockSpec(memory_space=pl.ANY)
    return pl.pallas_call(
        functools.partial(kernel, nz, na),
        out_shape=(
            jax.ShapeDtypeStruct((rows, cols), bf),
            jax.ShapeDtypeStruct((width, depth), bf),
        ),
        in_specs=[hbm, hbm, hbm, vmem, vmem],
        out_specs=(vmem, vmem),
        scratch_shapes=[
            pltpu.VMEM((nz, local, cols), bf),
            pltpu.VMEM((nz, local, width), bf),
            pltpu.VMEM((nz, local, depth), bf),
            pltpu.VMEM((rows, nz * width), bf),
            pltpu.VMEM((depth, cols), f4),
            pltpu.VMEM((depth, cols), bf),
            pltpu.VMEM((width, depth), f4),
            pltpu.VMEM((nc, rows, cols), f4),
            pltpu.VMEM((nc, rows, cols), bf),
            pltpu.VMEM((nc, rows, cols), bf),
            pltpu.VMEM((nc, rows, cols), bf),
            pltpu.VMEM((nc, rows, cols), bf),
            pltpu.VMEM((2 * rows, cols // CHUNKS), f4),
            dma((4,)),
            dma((2, nz)),
            dma((2, nz)),
            dma((nz,)),
            dma((nz,)),
            dma((nz,)),
            dma((2, nz, nc)),
            dma((2, nz, nc)),
            dma((2, nz, nc)),
            dma((2, nz, nc)),
            dma((CHUNKS,)),
            dma((CHUNKS,)),
            dma((CHUNKS, nc)),
            dma((CHUNKS, nc)),
        ],
        compiler_params=pltpu.CompilerParams(
            collective_id=0, has_side_effects=True, vmem_limit_bytes=64 * 1024 * 1024
        ),
    )(wavefunction, dressed_ops, site_tensor, old_sector[:, None], new_sector[None, :])


def solution(mesh):
    placed = (P("sec", None), P("sec", "aux"), P("sec", None), P("sec"), P())
    return jax.shard_map(
        functools.partial(body, mesh.shape["sec"], mesh.shape["aux"]),
        mesh=mesh,
        in_specs=placed,
        out_specs=(P(("sec", "aux"), None), P("sec", "aux")),
        check_vma=False,
    )
```

time: 562 us -> 209 us (0.37)
  blocking collectives: 513 us -> 0 us
  Pallas kernels: 0 us -> 202 us
  matrix products: 27.6 us -> 0 us
  between operations: 14 us -> 0.64 us
    psum x2 -> x0, blocking collectives: 513 us -> none  [the longest x1 344 us: body(): images = lax.psum(partial_images, 'sec')]
    pallas_call x0 -> x1, Pallas kernels: none -> 202 us  [body(): pl.pallas_call(functools.partial(kernel, nz, na), out_shape=(jax.ShapeDty...]
    dot_general x3 -> x0, matrix products: 27.6 us -> none  [the longest x1 12.7 us: body(): lax.dot_general(site_blocks, dressed_ops, (((0,), (0,)), ((), ())), prefe...]
  transfers between devices with their start and end apart: 1 -> 0, of which waited for: 0 -> 0; matrix products, arithmetic and copies ran while one was open for 3% -> 0% of each run, Pallas kernels for 0% -> 0%
where the time goes in v1:
time: 209 us
  Pallas kernels  202 us (97%)
  local copies, waits for them, and re-layouts  6.07 us (3%)
    pallas_call x1, Pallas kernels, body(): pl.pallas_call(functools.partial(kernel, nz, na), out_shape=(jax.ShapeDty...  202 us
    unnamed x2, local copies, waits for them, and re-layouts  4.37 us

profile of v1, /device:TPU:0, one launch (start us, length us, event | category | flops | bytes accessed | tf_op | source)
XLA Modules:
  0.0 208.9 jit_solution(13410579855621798455)
XLA Ops:
  0.6 1.7 copy.7.old_ref
  2.3 202.2 %shard_map.68 = (bf16[128,2048]{1,0:T(8,128)(2,1)}, bf16[1024,640]{1,0:T(8,128)(2,1)}) custom-call(bf16[1024,2048]{1,0:T(8,128)(2,1)} %w_ref.1, bf16[1024,640]{1,0:T(8,128)(2,1)} %d_ref.1, bf16[1024,4096]{1,0:T(8,128)(2,1)} %s_ref.1, s32[1024,1]{1,0:T(8,128)} %copy.7.old_ref, s32[1,4096]{1,0:T(1,128)} %bitcast.2), custom_call_target="tpu_custom_call" | custom-call | tf_op jit(solution)/shard_map/pallas_call | solution.py:294
  204.6 1.9 copy.10
  206.4 2.5 %copy.11 = bf16[1024,640]{1,0:T(8,128)(2,1)} copy(bf16[1024,640]{1,0:T(8,128)(2,1)} %get-tuple-element.5) | data formatting | bytes 2621440

commit v2 on v1

--- a/solution.py
+++ b/solution.py
@@ -18,7 +18,7 @@
 def kernel(
     nz, na, w_ref, d_ref, s_ref, old_ref, new_ref, sig_ref, rot_ref,
     wf, sf, df, sm, acc, img, rotacc, keep, msend, mrecv, ssend, srecv, tmp,
-    loc, z_s, z_r, dr_s, dl_s, d_r, p_s, p_r, m_s, m_r, x_s, x_r, y_s, y_r,
+    loc, z_s, z_r, wr_s, wl_s, w_r, dr_s, dl_s, d_r, p_s, p_r, m_s, m_r, x_s, x_r, y_s, y_r,
 ):
     nc = na // 2
     z = lax.axis_index("sec")
@@ -68,52 +68,87 @@
             src_ref=src, dst_ref=dst, send_sem=send, recv_sem=recv, device_id=where, device_id_type=MESH
         )
 
-    def z_copy(kind, k):
+    full = (wf, sf)
+
+    def s_copy(k):
         t = lax.rem(z + k, nz)
-        if kind == 0:
-            src, dst = w_ref.at[mine], wf.at[z, mine]
-        else:
-            src, dst = sm.at[:, block(t)], sf.at[z, mine]
-        return remote(src, dst, z_s.at[kind, k], z_r.at[kind, k], {"sec": t})
-
-    full = (wf, sf)
-
-    def z_arrived(kind, k):
+        return remote(sm.at[:, block(t)], sf.at[z, mine], z_s.at[k], z_r.at[k], {"sec": t})
+
+    def s_arrived(k):
         p = lax.rem(z + nz - k, nz)
+        ref = sf.at[p, mine]
+        remote(ref, ref, z_s.at[k], z_r.at[k], {"sec": p}).wait_recv()
+
+    def p_copy(kind, p, k):
         ref = full[kind].at[p, mine]
-        remote(ref, ref, z_s.at[kind, k], z_r.at[kind, k], {"sec": p}).wait_recv()
-
-    def p_copy(kind, j, k):
-        ref = full[kind].at[lax.rem(z + nz - j, nz), mine]
-        return remote(ref, ref, p_s.at[kind, j, k], p_r.at[kind, j, k], {"aux": peer(k)})
-
-    def p_arrived(kind, j, k):
-        ref = full[kind].at[lax.rem(z + nz - j, nz), part(back(k))]
-        remote(ref, ref, p_s.at[kind, j, k], p_r.at[kind, j, k], {"aux": back(k)}).wait_recv()
-
-    def m_copy(kind, j, k):
-        ref = full[kind].at[lax.rem(z + nz - j, nz), part(back(k))]
-        return remote(ref, ref, m_s.at[kind, j, k], m_r.at[kind, j, k], {"aux": mate})
-
-    def m_arrived(kind, j, k):
+        return remote(ref, ref, p_s.at[kind, p, k], p_r.at[kind, p, k], {"aux": peer(k)})
+
+    def p_arrived(kind, p, k):
+        ref = full[kind].at[p, part(back(k))]
+        remote(ref, ref, p_s.at[kind, p, k], p_r.at[kind, p, k], {"aux": back(k)}).wait_recv()
+
+    def m_copy(kind, p, k):
+        ref = full[kind].at[p, part(back(k))]
+        return remote(ref, ref, m_s.at[kind, p, k], m_r.at[kind, p, k], {"aux": mate})
+
+    def m_arrived(kind, p, k):
         theirs = lax.rem(mate + na - 2 * k, na)
-        ref = full[kind].at[lax.rem(z + nz - j, nz), part(theirs)]
-        remote(ref, ref, m_s.at[kind, j, k], m_r.at[kind, j, k], {"aux": mate}).wait_recv()
-
-    def spread(kind, j):
-        z_arrived(kind, j)
+        ref = full[kind].at[p, part(theirs)]
+        remote(ref, ref, m_s.at[kind, p, k], m_r.at[kind, p, k], {"aux": mate}).wait_recv()
+
+    def spread(kind, p):
         for k in range(1, nc):
-            p_copy(kind, j, k).start()
-        m_copy(kind, j, 0).start()
-
-    def relay(kind, j):
+            p_copy(kind, p, k).start()
+        m_copy(kind, p, 0).start()
+
+    def relay(kind, p):
         for k in range(1, nc):
-            p_arrived(kind, j, k)
-            m_copy(kind, j, k).start()
-
-    def landed(kind, j):
+            p_arrived(kind, p, k)
+            m_copy(kind, p, k).start()
+
+    def landed(kind, p):
         for k in range(nc):
-            m_arrived(kind, j, k)
+            m_arrived(kind, p, k)
+
+    def sides(distance, act):
+        @pl.when(z - distance >= 0)
+        def _():
+            act(z - distance)
+
+        @pl.when(z + distance < nz)
+        def _():
+            act(z + distance)
+
+    def w_right(p, src):
+        return remote(src, wf.at[p, mine], wr_s.at[p], w_r.at[p], {"sec": z + 1})
+
+    def w_left(p, src):
+        return remote(src, wf.at[p, mine], wl_s.at[p], w_r.at[p], {"sec": z - 1})
+
+    def w_step(distance):
+        @pl.when(z - distance >= 0)
+        def _():
+            p = z - distance
+            ref = wf.at[p, mine]
+            remote(ref, ref, wr_s.at[p], w_r.at[p], {"sec": z - 1}).wait_recv()
+
+            @pl.when(z < nz - 1)
+            def _():
+                w_right(p, ref).start()
+
+            spread(0, p)
+
+        @pl.when(z + distance < nz)
+        def _():
+            p = z + distance
+            ref = wf.at[p, mine]
+            remote(ref, ref, wl_s.at[p], w_r.at[p], {"sec": z + 1}).wait_recv()
+
+            @pl.when(z > 0)
+            def _():
+                w_left(p, ref).start()
+
+            spread(0, p)
 
     def d_right(p):
         return remote(df.at[p], df.at[p], dr_s.at[p], d_r.at[p], {"sec": z + 1})
@@ -140,17 +175,14 @@
             def _():
                 d_left(p).start()
 
-    for k in range(1, nz):
-        z_copy(0, k).start()
-    loads[1].wait()
-
     @pl.when(z < nz - 1)
     def _():
-        d_right(z).start()
+        w_right(z, w_ref.at[mine]).start()
 
     @pl.when(z > 0)
     def _():
-        d_left(z).start()
+        w_left(z, w_ref.at[mine]).start()
+
 
     loads[0].wait()
     for t in range(nz):
@@ -159,7 +191,16 @@
         allowed = (offset >= 0) & (offset <= 2)
         sm[:, band] = jnp.where(allowed, sm[:, band].astype(jnp.float32), 0.0).astype(jnp.bfloat16)
     for k in range(1, nz):
-        z_copy(1, k).start()
+        s_copy(k).start()
+    loads[1].wait()
+
+    @pl.when(z < nz - 1)
+    def _():
+        d_right(z).start()
+
+    @pl.when(z > 0)
+    def _():
+        d_left(z).start()
 
     loads[3].wait()
 
@@ -187,31 +228,37 @@
             rotacc[r, :] = term if first else rotacc[r, :] + term
 
     add_images(z, True)
+    w_step(1)
     add_rotated(z, True)
-
-    near = [1, nz - 1] + list(range(2, nz - 1))
-    for j in near:
-        spread(0, j)
+    w_step(2)
+    sides(1, lambda p: relay(0, p))
     d_step(1)
-    for j in near:
-        spread(1, j)
-    for j in near:
-        relay(0, j)
+    for d in range(3, nz):
+        w_step(d)
+    others = [lax.rem(z + nz - j, nz) for j in range(1, nz)]
+    for j in range(1, nz):
+        s_arrived(j)
+        spread(1, others[j - 1])
     for d in range(2, nz):
+        sides(d, lambda p: relay(0, p))
+    for d in range(2, nz - 1):
         d_step(d)
-        if d == 2:
-            for j in near:
-                relay(1, j)
-            for j in near:
-                landed(0, j)
-
-    for j in range(1, nz):
-        add_images(lax.rem(z + nz - j, nz), False)
-
-    @pl.loop(0, CHUNKS)
-    def _(i):
-        r = pl.ds(pl.multiple_of(i * step, step), step)
-        img[:, r] = acc[:, r].astype(jnp.bfloat16)
+    for p in others:
+        relay(1, p)
+
+    def images_of(p):
+        landed(0, p)
+        add_images(p, False)
+
+    for d in range(1, nz - 1):
+        sides(d, images_of)
+    for p in others:
+        landed(1, p)
+    for d in range(1, nz - 1):
+        sides(d, lambda p: add_rotated(p, False))
+    if nz > 2:
+        d_step(nz - 1)
+    sides(nz - 1, lambda p: landed(0, p))
 
     def x_copy(i):
         r = pl.ds(i * step, step)
@@ -223,6 +270,12 @@
 
     def terms(i):
         r = pl.ds(i * step, step)
+
+        def last(p):
+            acc[:, r] = acc[:, r] + tdot(df[p], wf[p, :, r])
+
+        sides(nz - 1, last)
+        img[:, r] = acc[:, r].astype(jnp.bfloat16)
 
         @pl.loop(0, nc)
         def _(b):
@@ -247,10 +300,7 @@
             combine(i - 1)
     combine(CHUNKS - 1)
 
-    for j in near:
-        landed(1, j)
-    for j in range(1, nz):
-        add_rotated(lax.rem(z + nz - j, nz), False)
+    sides(nz - 1, lambda p: add_rotated(p, False))
     rot_ref[...] = rotacc[...].astype(jnp.bfloat16)
 
     for i in range(CHUNKS):
@@ -261,21 +311,23 @@
             total = total + srecv[k, :, r].astype(jnp.float32)
         sig_ref[:, r] = total.astype(jnp.bfloat16)
 
-    for kind in range(2):
-        for j in range(1, nz):
-            z_copy(kind, j).wait_send()
+    for j in range(1, nz):
+        s_copy(j).wait_send()
+        for kind in range(2):
             for k in range(1, nc):
-                p_copy(kind, j, k).wait_send()
+                p_copy(kind, others[j - 1], k).wait_send()
             for k in range(nc):
-                m_copy(kind, j, k).wait_send()
+                m_copy(kind, others[j - 1], k).wait_send()
     for p in range(nz):
         @pl.when((p <= z) & (z < nz - 1))
         def _():
             d_right(p).wait_send()
+            w_right(p, wf.at[p, mine]).wait_send()
 
         @pl.when((p >= z) & (z > 0))
         def _():
             d_left(p).wait_send()
+            w_left(p, wf.at[p, mine]).wait_send()
     for i in range(CHUNKS):
         x_copy(i).wait_send()
         for k in range(1, nc):
@@ -314,8 +366,11 @@
             pltpu.VMEM((nc, rows, cols), bf),
             pltpu.VMEM((2 * rows, cols // CHUNKS), f4),
             dma((4,)),
-            dma((2, nz)),
-            dma((2, nz)),
+            dma((nz,)),
+            dma((nz,)),
+            dma((nz,)),
+            dma((nz,)),
+            dma((nz,)),
             dma((nz,)),
             dma((nz,)),
             dma((nz,)),

time: 209 us -> 207 us (level)
    pallas_call x1, Pallas kernels: 202 us -> 200 us  [body(): pl.pallas_call(functools.partial(kernel, nz, na), out_shape=(jax.ShapeDty...]
where the time goes in v2:
time: 207 us; the launch traced here: 206 us
  Pallas kernels  200 us (97%)
  local copies, waits for them, and re-layouts  6.07 us (3%)
    pallas_call x1, Pallas kernels, body(): pl.pallas_call(functools.partial(kernel, nz, na), out_shape=(jax.ShapeDty...  200 us
    unnamed x2, local copies, waits for them, and re-layouts  4.37 us

profile of v2, /device:TPU:0, one launch (start us, length us, event | category | flops | bytes accessed | tf_op | source)
XLA Modules:
  0.0 206.4 jit_solution(1037273195464464379)
XLA Ops:
  0.6 1.7 copy.7.old_ref
  2.3 199.7 %shard_map.68 = (bf16[128,2048]{1,0:T(8,128)(2,1)}, bf16[1024,640]{1,0:T(8,128)(2,1)}) custom-call(bf16[1024,2048]{1,0:T(8,128)(2,1)} %w_ref.1, bf16[1024,640]{1,0:T(8,128)(2,1)} %d_ref.1, bf16[1024,4096]{1,0:T(8,128)(2,1)} %s_ref.1, s32[1024,1]{1,0:T(8,128)} %copy.7.old_ref, s32[1,4096]{1,0:T(1,128)} %bitcast.2), custom_call_target="tpu_custom_call" | custom-call | tf_op jit(solution)/shard_map/pallas_call | solution.py:346
  202.0 1.9 copy.10
  203.9 2.5 %copy.11 = bf16[1024,640]{1,0:T(8,128)(2,1)} copy(bf16[1024,640]{1,0:T(8,128)(2,1)} %get-tuple-element.5) | data formatting | bytes 2621440

commit v3 on v2

--- a/solution.py
+++ b/solution.py
@@ -231,7 +231,6 @@
     w_step(1)
     add_rotated(z, True)
     w_step(2)
-    sides(1, lambda p: relay(0, p))
     d_step(1)
     for d in range(3, nz):
         w_step(d)
@@ -239,10 +238,10 @@
     for j in range(1, nz):
         s_arrived(j)
         spread(1, others[j - 1])
-    for d in range(2, nz):
-        sides(d, lambda p: relay(0, p))
     for d in range(2, nz - 1):
         d_step(d)
+    for d in range(1, nz):
+        sides(d, lambda p: relay(0, p))
     for p in others:
         relay(1, p)
 

time: 207 us -> 207 us (level)
  no operation moved by 1% of the time
where the time goes in v3:
time: 207 us; the launch traced here: 206 us
  Pallas kernels  200 us (97%)
  local copies, waits for them, and re-layouts  6.07 us (3%)
    pallas_call x1, Pallas kernels, body(): pl.pallas_call(functools.partial(kernel, nz, na), out_shape=(jax.ShapeDty...  200 us
    unnamed x2, local copies, waits for them, and re-layouts  4.37 us

profile of v3, /device:TPU:0, one launch (start us, length us, event | category | flops | bytes accessed | tf_op | source)
XLA Modules:
  0.0 206.4 jit_solution(2951028012147653891)
XLA Ops:
  0.6 1.7 copy.7.old_ref
  2.3 199.7 %shard_map.68 = (bf16[128,2048]{1,0:T(8,128)(2,1)}, bf16[1024,640]{1,0:T(8,128)(2,1)}) custom-call(bf16[1024,2048]{1,0:T(8,128)(2,1)} %w_ref.1, bf16[1024,640]{1,0:T(8,128)(2,1)} %d_ref.1, bf16[1024,4096]{1,0:T(8,128)(2,1)} %s_ref.1, s32[1024,1]{1,0:T(8,128)} %copy.7.old_ref, s32[1,4096]{1,0:T(1,128)} %bitcast.2), custom_call_target="tpu_custom_call" | custom-call | tf_op jit(solution)/shard_map/pallas_call | solution.py:345
  202.0 1.9 copy.10
  203.9 2.5 %copy.11 = bf16[1024,640]{1,0:T(8,128)(2,1)} copy(bf16[1024,640]{1,0:T(8,128)(2,1)} %get-tuple-element.5) | data formatting | bytes 2621440

commit v4 on v3

--- a/solution.py
+++ b/solution.py
@@ -150,11 +150,11 @@
 
             spread(0, p)
 
-    def d_right(p):
-        return remote(df.at[p], df.at[p], dr_s.at[p], d_r.at[p], {"sec": z + 1})
-
-    def d_left(p):
-        return remote(df.at[p], df.at[p], dl_s.at[p], d_r.at[p], {"sec": z - 1})
+    def d_right(p, src=None):
+        return remote(df.at[p] if src is None else src, df.at[p], dr_s.at[p], d_r.at[p], {"sec": z + 1})
+
+    def d_left(p, src=None):
+        return remote(df.at[p] if src is None else src, df.at[p], dl_s.at[p], d_r.at[p], {"sec": z - 1})
 
     def d_step(distance):
         @pl.when(z - distance >= 0)
@@ -190,18 +190,6 @@
         offset = new_ref[:, band] - old_ref[mine, :]
         allowed = (offset >= 0) & (offset <= 2)
         sm[:, band] = jnp.where(allowed, sm[:, band].astype(jnp.float32), 0.0).astype(jnp.bfloat16)
-    for k in range(1, nz):
-        s_copy(k).start()
-    loads[1].wait()
-
-    @pl.when(z < nz - 1)
-    def _():
-        d_right(z).start()
-
-    @pl.when(z > 0)
-    def _():
-        d_left(z).start()
-
     loads[3].wait()
 
     @pl.loop(0, local // 128)
@@ -227,12 +215,24 @@
             term = tdot(sf[p, :, r], df[p])
             rotacc[r, :] = term if first else rotacc[r, :] + term
 
+    w_step(1)
+    for d in range(2, nz - 1):
+        w_step(d)
+    @pl.when(z < nz - 1)
+    def _():
+        d_right(z, d_ref).start()
+
+    @pl.when(z > 0)
+    def _():
+        d_left(z, d_ref).start()
+
+    for k in range(1, nz):
+        s_copy(k).start()
+    loads[1].wait()
     add_images(z, True)
-    w_step(1)
     add_rotated(z, True)
-    w_step(2)
     d_step(1)
-    for d in range(3, nz):
+    for d in range(max(2, nz - 1), nz):
         w_step(d)
     others = [lax.rem(z + nz - j, nz) for j in range(1, nz)]
     for j in range(1, nz):

time: 207 us -> 190 us (0.918)
  Pallas kernels: 200 us -> 183 us
    pallas_call x1, Pallas kernels: 200 us -> 183 us  [body(): pl.pallas_call(functools.partial(kernel, nz, na), out_shape=(jax.ShapeDty...]
where the time goes in v4:
time: 190 us
  Pallas kernels  183 us (96%)
  local copies, waits for them, and re-layouts  6.07 us (3%)
    pallas_call x1, Pallas kernels, body(): pl.pallas_call(functools.partial(kernel, nz, na), out_shape=(jax.ShapeDty...  183 us
    unnamed x2, local copies, waits for them, and re-layouts  4.37 us

profile of v4, /device:TPU:0, one launch (start us, length us, event | category | flops | bytes accessed | tf_op | source)
XLA Modules:
  0.0 189.8 jit_solution(6495776238731635593)
XLA Ops:
  0.6 1.7 copy.7.old_ref
  2.3 183.1 %shard_map.68 = (bf16[128,2048]{1,0:T(8,128)(2,1)}, bf16[1024,640]{1,0:T(8,128)(2,1)}) custom-call(bf16[1024,2048]{1,0:T(8,128)(2,1)} %w_ref.1, bf16[1024,640]{1,0:T(8,128)(2,1)} %d_ref.1, bf16[1024,4096]{1,0:T(8,128)(2,1)} %s_ref.1, s32[1024,1]{1,0:T(8,128)} %copy.7.old_ref, s32[1,4096]{1,0:T(1,128)} %bitcast.2), custom_call_target="tpu_custom_call" | custom-call | tf_op jit(solution)/shard_map/pallas_call | solution.py:345
  185.4 1.9 copy.10
  187.3 2.5 %copy.11 = bf16[1024,640]{1,0:T(8,128)(2,1)} copy(bf16[1024,640]{1,0:T(8,128)(2,1)} %get-tuple-element.5) | data formatting | bytes 2621440
